TPU v7x, 256 devices: a whole 4x4x8 slice. The times are simulated.
256 devices in a mesh: tm: 8 (over z), space: 32 (over y, x, core).
Axes of the slice: x: 4, y: 4, z: 8, core: 2. Of those that a mesh axis runs over, the one named last changes fastest.
Arguments:
- features: bfloat16 [16, 256, 80, 256], P('tm', 'space'), may hold values from -24 to 24
- conv_weights: bfloat16 [2, 3, 3, 3, 256, 256], replicated, may hold values from -0.078125 to 0.078125
- conv_bias: float32 [2, 256], replicated, may hold values from -3 to 3
- norm_gain: float32 [2, 256], replicated, may hold values from 0.1 to 1.9
- norm_shift: float32 [2, 256], replicated, may hold values from -3 to 3
Outputs:
- block_out: bfloat16 [16, 256, 80, 256], P('tm', 'space')
All inputs are finite; a program needn't handle non-finite values.
Results may differ from a plain program's by a relative error of at most 0.008.
Values may be sent and summed in bfloat16 or wider, within the bound.
A program may use at most 64 MiB of HBM per device.

v0:
```python
import jax
import jax.numpy as jnp
from jax import lax
from jax.sharding import PartitionSpec as P

GROUPS = 32


def passed_along(shard, axis, by):
    length = lax.axis_size(axis)
    pairs = [(i, i + by) for i in range(length) if 0 <= i + by < length]
    return lax.ppermute(shard, axis, pairs)


def with_halo(block, sides, width):
    for axis, dim in sides:
        count = lax.axis_size(axis)
        forward = [(i, i + 1) for i in range(count - 1)]
        backward = [(target, source) for source, target in forward]
        low = lax.ppermute(
            lax.slice_in_dim(block, block.shape[dim] - width, None, axis=dim), axis, forward
        )
        high = lax.ppermute(lax.slice_in_dim(block, 0, width, axis=dim), axis, backward)
        block = jnp.concatenate([low, block, high], axis=dim)
    return block


def group_norm(field, gain, shift):
    frames, rows, columns, chans = field.shape
    grouped = field.reshape(frames, rows, columns, GROUPS, chans // GROUPS)
    count = (
        frames * rows * columns * (chans // GROUPS) * lax.axis_size("tm") * lax.axis_size("space")
    )
    totals = lax.psum(jnp.sum(grouped, axis=(0, 1, 2, 4)), ("tm", "space"))
    average = totals / count
    centered = grouped - average[:, None]
    spread = lax.psum(jnp.sum(centered * centered, axis=(0, 1, 2, 4)), ("tm", "space"))
    variance = spread / count
    normed = centered / jnp.sqrt(variance + 1e-06)[:, None]
    normed = normed.reshape(frames, rows, columns, chans) * gain + shift
    return jax.nn.silu(normed).astype(jnp.bfloat16)


def causal_conv(normed, weights, bias, first_device):
    frames, rows, columns, chans = normed.shape
    earlier = passed_along(normed, "tm", 1)
    earlier = jnp.where(first_device, jnp.concatenate([normed[:1], normed[:1]], 0), earlier)
    extended = jnp.concatenate([earlier, normed], 0)
    padded = with_halo(extended, (("space", 1),), 1)
    padded = jnp.pad(padded, ((0, 0), (0, 0), (1, 1), (0, 0)))
    total = jnp.zeros((frames * rows * columns, chans), jnp.float32)
    for offset_t in range(3):
        for offset_h in range(3):
            patch = jnp.concatenate(
                [
                    padded[
                        offset_t : offset_t + frames,
                        offset_h : offset_h + rows,
                        shift_w : shift_w + columns,
                    ]
                    for shift_w in range(3)
                ],
                -1,
            )
            total = total + jnp.dot(
                patch.reshape(frames * rows * columns, 3 * chans),
                weights[offset_t, offset_h].reshape(3 * chans, chans),
                preferred_element_type=jnp.float32,
            )
    return total.reshape(frames, rows, columns, chans) + bias


def shards(features, conv_weights, conv_bias, norm_gain, norm_shift):
    first_device = lax.axis_index("tm") == 0
    first = group_norm(features.astype(jnp.float32), norm_gain[0], norm_shift[0])
    middle = causal_conv(first, conv_weights[0], conv_bias[0], first_device).astype(jnp.bfloat16)
    second = group_norm(middle.astype(jnp.float32), norm_gain[1], norm_shift[1])
    result = features.astype(jnp.float32) + causal_conv(
        second, conv_weights[1], conv_bias[1], first_device
    )
    return result.astype(jnp.bfloat16)


def solution(mesh):
    placed = (P("tm", "space", None, None), P(), P(), P(), P())
    return jax.shard_map(
        shards, mesh=mesh, in_specs=placed, out_specs=P("tm", "space", None, None), check_vma=False
    )
```

profile of v0, /device:TPU:1, one launch (start us, length us, event | category | flops | bytes accessed | tf_op | source)
XLA Modules:
  0.0 398.8 jit_solution(16281773525877225152)
XLA Ops:
  0.0 1.3 convert_reduce_fusion
  1.5 0.8 fusion.32
  2.2 81.4 %psum.28 = f32[32]{0:T(128)S(1)} all-reduce(f32[32]{0:T(128)S(1)} %reduce_sum.51), channel_id=1, replica_groups=mesh['tm'=8,'space'=32] {'tm','space'}, use_global_device_ids=true, to_apply=%region_2.0 | all-reduce | flops 32 | bytes 256 | tf_op jit(solution)/shard_map/psum | solution.py:34
  83.8 1.3 fusion.17
  85.3 0.8 fusion.33
  86.1 72.4 %psum.29 = f32[32]{0:T(128)S(1)} all-reduce(f32[32]{0:T(128)S(1)} %reduce_sum.54), channel_id=1, replica_groups=mesh['tm'=8,'space'=32] {'tm','space'}, use_global_device_ids=true, to_apply=%region_5.6 | all-reduce | flops 32 | bytes 256 | tf_op jit(solution)/shard_map/psum | solution.py:37
  158.6 1.5 multiply_convert_fusion.1
  160.2 4.5 %collective-permute-start = (bf16[2,8,80,256]{3,2,1,0:T(8,128)(2,1)S(1)}, bf16[2,8,80,256]{3,2,1,0:T(8,128)(2,1)}, u32[]{:S(2)}, u32[]{:S(2)}) collective-permute-start(bf16[2,8,80,256]{3,2,1,0:T(8,128)(2,1)S(1)} %multiply_convert_fusion.1), channel_id=1, source_target_pairs={{0,32},{32,64},{64,96},{96,128},{128,160},{160,192},{192,224},{1,3... | collective-permute-start | bytes 1966088 | tf_op jit(solution)/shard_map/ppermute | solution.py:12
  164.7 6.8 %slice_bitcast_fusion = (bf16[3,3,3,256,256]{4,3,2,1,0:T(8,128)(2,1)}, bf16[3,3,3,256,256]{4,3,2,1,0:T(8,128)(2,1)}) fusion(bf16[2,3,3,3,256,256]{5,4,3,2,1,0:T(8,128)(2,1)} %param.6), kind=kLoop, calls=%fused_computation.3 | loop fusion | bytes 14155776 | tf_op jit(solution)/shard_map/squeeze | solution.py:79
  171.5 0.8 slice.370
  172.3 4.6 %fusion.23 = (bf16[1,1,3,256,256]{4,3,2,1,0:T(8,128)(2,1)S(1)}, bf16[1,1,3,256,256]{4,3,2,1,0:T(8,128)(2,1)S(1)}, bf16[1,1,3,256,256]{4,3,2,1,0:T(8,128)(2,1)S(1...) fusion(bf16[3,3,3,256,256]{4,3,2,1,0:T(8,128)(2,1)} %get-tuple-, ...), kind=kLoop, calls=%fused_computation.86 | loop fusion | bytes 14155776 | tf_op jit(solution)/shard_map/slice | solution.py:67
  177.4 3.7 collective-permute-start.1
  181.1 2.1 collective-permute-start.2
  183.3 4.4 %collective-permute-done.2 = bf16[4,1,80,256]{3,2,1,0:T(8,128)(2,1)S(1)} collective-permute-done((bf16[4,1,80,256]{3,2,1,0:T(8,128)(2,1)S(1)}, bf16[4,1,80,256]{3,2,1,0:T(8,128)(2,1)S(1)}, u32[]{:S(2)}, u32[]{:S(2)}) %collective-permute-start.2) | collective-permute-done | bytes 163872 | tf_op jit(solution)/shard_map/ppermute | solution.py:23
  187.7 0.8 fusion.12
  188.5 4.1 %fusion.26 = (bf16[2,8,80,256]{3,2,1,0:T(8,128)(2,1)S(1)}, bf16[2,8,80,256]{3,2,1,0:T(8,128)(2,1)S(1)}, bf16[2,8,80,256]{3,2,1,0:T(8,128)(2,1)S(1)}, bf16[2,8,80...) fusion(bf16[4,10,82,256]{3,2,1,0:T(8,128)(2,1)S(1)} %fusion.12), kind=kLoop, calls=%fused_computation.89 | loop fusion | bytes 23592960 | tf_op jit(solution)/shard_map/slice | solution.py:56
  195.9 0.7 convolution_add_fusion.14
  196.7 0.7 convolution_add_fusion.13
  200.2 0.7 convert_reduce_fusion.1
  201.1 78.2 %psum.30 = f32[32]{0:T(128)S(1)} all-reduce(f32[32]{0:T(128)S(1)} %reduce_sum.72), channel_id=1, replica_groups=mesh['tm'=8,'space'=32] {'tm','space'}, use_global_device_ids=true, to_apply=%region_8.9 | all-reduce | flops 32 | bytes 256 | tf_op jit(solution)/shard_map/psum | solution.py:34
  279.9 74.3 %psum.31 = f32[32]{0:T(128)S(1)} all-reduce(f32[32]{0:T(128)S(1)} %reduce_sum.75), channel_id=1, replica_groups=mesh['tm'=8,'space'=32] {'tm','space'}, use_global_device_ids=true, to_apply=%region_11.12 | all-reduce | flops 32 | bytes 256 | tf_op jit(solution)/shard_map/psum | solution.py:37
  354.9 3.0 collective-permute-start.3
  357.9 13.3 %collective-permute-done.3 = bf16[2,8,80,256]{3,2,1,0:T(8,128)(2,1)S(1)} collective-permute-done((bf16[2,8,80,256]{3,2,1,0:T(8,128)(2,1)S(1)}, bf16[2,8,80,256]{3,2,1,0:T(8,128)(2,1)S(1)}, u32[]{:S(2)}, u32[]{:S(2)}) %collective-permute-start.3) | collective-permute-done | bytes 655392 | tf_op jit(solution)/shard_map/ppermute | solution.py:12
  371.4 4.3 %collective-permute-start.4 = (bf16[4,1,80,256]{3,2,1,0:T(8,128)(2,1)S(1)}, bf16[4,1,80,256]{3,2,1,0:T(8,128)(2,1)S(1)}, u32[]{:S(2)}, u32[]{:S(2)}) collective-permute-start(bf16[4,1,80,256]{3,2,1,0:T(8,128)(2,1)S(1)} %get-tuple-element.75), channel_id=1, source_target_pairs={{0,1},{1,2},{2,3},{3,4},{4,5},{5,6},{6,7},{7,8},{8,9},{9,10},{10,1... | collective-permute-start | bytes 491528 | tf_op jit(solution)/shard_map/ppermute | solution.py:20
  375.7 1.9 collective-permute-start.5
  377.9 4.4 %collective-permute-done.5 = bf16[4,1,80,256]{3,2,1,0:T(8,128)(2,1)S(1)} collective-permute-done((bf16[4,1,80,256]{3,2,1,0:T(8,128)(2,1)S(1)}, bf16[4,1,80,256]{3,2,1,0:T(8,128)(2,1)S(1)}, u32[]{:S(2)}, u32[]{:S(2)}) %collective-permute-start.5) | collective-permute-done | bytes 163872 | tf_op jit(solution)/shard_map/ppermute | solution.py:23
  382.9 0.8 select_maximum_fusion
  383.7 4.1 %fusion.25 = (bf16[2,8,80,256]{3,2,1,0:T(8,128)(2,1)S(1)}, bf16[2,8,80,256]{3,2,1,0:T(8,128)(2,1)S(1)}, bf16[2,8,80,256]{3,2,1,0:T(8,128)(2,1)S(1)}, bf16[2,8,80...) fusion(bf16[4,10,82,256]{3,2,1,0:T(8,128)(2,1)S(1)} %select_max, ...), kind=kLoop, calls=%fused_computation.88 | loop fusion | bytes 23592960 | tf_op jit(solution)/shard_map/slice | solution.py:56
  388.0 0.8 copy-done.4
  396.0 0.7 convolution_add_fusion.1
  396.7 0.7 convolution_add_fusion
  397.8 1.0 fusion.22
  (76 shorter events, 17.3 us)
Async XLA Ops:
  160.2 17.1 %collective-permute-start = (bf16[2,8,80,256]{3,2,1,0:T(8,128)(2,1)S(1)}, bf16[2,8,80,256]{3,2,1,0:T(8,128)(2,1)}, u32[]{:S(2)}, u32[]{:S(2)}) collective-permute-start(bf16[2,8,80,256]{3,2,1,0:T(8,128)(2,1)S(1)} %multiply_convert_fusion.1), channel_id=1, source_target_pairs={{0,32},{32,64},{64,96},{96,128},{128,160},{160,192},{192,224},{1,3... | collective-permute-start | bytes 1966088 | tf_op jit(solution)/shard_map/ppermute | solution.py:12
  172.3 5.0 %copy-start.5 = (bf16[1,8,80,256]{3,2,1,0:T(8,128)(2,1)S(1)}, bf16[1,8,80,256]{3,2,1,0:T(8,128)(2,1)}, u32[]{:S(2)}) copy-start(bf16[1,8,80,256]{3,2,1,0:T(8,128)(2,1)} %slice.370) | copy-start | bytes 983044
  176.9 6.3 %copy-start.6 = (f32[2,256]{1,0:T(2,128)S(1)}, f32[2,256]{1,0:T(2,128)}, u32[]{:S(2)}) copy-start(f32[2,256]{1,0:T(2,128)} %param.7) | copy-start | bytes 6148
  177.4 6.0 %collective-permute-start.1 = (bf16[4,1,80,256]{3,2,1,0:T(8,128)(2,1)S(1)}, bf16[4,1,80,256]{3,2,1,0:T(8,128)(2,1)S(1)}, u32[]{:S(2)}, u32[]{:S(2)}) collective-permute-start(bf16[4,1,80,256]{3,2,1,0:T(8,128)(2,1)S(1)} %get-tuple-element.79), channel_id=1, source_target_pairs={{0,1},{1,2},{2,3},{3,4},{4,5},{5,6},{6,7},{7,8},{8,9},{9,10},{10,1... | collective-permute-start | bytes 491528 | tf_op jit(solution)/shard_map/ppermute | solution.py:20
  181.1 6.6 %collective-permute-start.2 = (bf16[4,1,80,256]{3,2,1,0:T(8,128)(2,1)S(1)}, bf16[4,1,80,256]{3,2,1,0:T(8,128)(2,1)S(1)}, u32[]{:S(2)}, u32[]{:S(2)}) collective-permute-start(bf16[4,1,80,256]{3,2,1,0:T(8,128)(2,1)S(1)} %get-tuple-element.80), channel_id=1, source_target_pairs={{1,0},{2,1},{3,2},{4,3},{5,4},{6,5},{7,6},{8,7},{9,8},{10,9},{11,1... | collective-permute-start | bytes 491528 | tf_op jit(solution)/shard_map/ppermute | solution.py:23
  354.9 16.3 %collective-permute-start.3 = (bf16[2,8,80,256]{3,2,1,0:T(8,128)(2,1)S(1)}, bf16[2,8,80,256]{3,2,1,0:T(8,128)(2,1)S(1)}, u32[]{:S(2)}, u32[]{:S(2)}) collective-permute-start(bf16[2,8,80,256]{3,2,1,0:T(8,128)(2,1)S(1)} %multiply_convert_fusion), channel_id=1, source_target_pairs={{0,32},{32,64},{64,96},{96,128},{128,160},{160,192},{192,224},{1,3... | collective-permute-start | bytes 1966088 | tf_op jit(solution)/shard_map/ppermute | solution.py:12
  371.4 6.5 %collective-permute-start.4 = (bf16[4,1,80,256]{3,2,1,0:T(8,128)(2,1)S(1)}, bf16[4,1,80,256]{3,2,1,0:T(8,128)(2,1)S(1)}, u32[]{:S(2)}, u32[]{:S(2)}) collective-permute-start(bf16[4,1,80,256]{3,2,1,0:T(8,128)(2,1)S(1)} %get-tuple-element.75), channel_id=1, source_target_pairs={{0,1},{1,2},{2,3},{3,4},{4,5},{5,6},{6,7},{7,8},{8,9},{9,10},{10,1... | collective-permute-start | bytes 491528 | tf_op jit(solution)/shard_map/ppermute | solution.py:20
  375.7 6.6 %collective-permute-start.5 = (bf16[4,1,80,256]{3,2,1,0:T(8,128)(2,1)S(1)}, bf16[4,1,80,256]{3,2,1,0:T(8,128)(2,1)S(1)}, u32[]{:S(2)}, u32[]{:S(2)}) collective-permute-start(bf16[4,1,80,256]{3,2,1,0:T(8,128)(2,1)S(1)} %get-tuple-element.76), channel_id=1, source_target_pairs={{1,0},{2,1},{3,2},{4,3},{5,4},{6,5},{7,6},{8,7},{9,8},{10,9},{11,1... | collective-permute-start | bytes 491528 | tf_op jit(solution)/shard_map/ppermute | solution.py:23
  387.8 1.0 copy-start.4
  390.2 1.0 copy-start.3
  391.2 1.0 copy-start.2
  392.2 1.0 copy-start.1
  396.7 1.1 copy-start
where the time goes:
time: 402 us; the launch traced here: 399 us
  blocking collectives  306 us (76%)
  local copies, waits for them, and re-layouts  25.8 us (6%)
  waiting for transfers between devices  22.9 us (6%)
  starting transfers between devices  19.5 us (5%)
  matrix products  12.5 us (3%)
  other arithmetic  11.3 us (3%)
    psum x2, blocking collectives, group_norm(): totals = lax.psum(jnp.sum(grouped, axis=(0, 1, 2, 4)), ('tm', 'space'))  160 us
    psum x2, blocking collectives, group_norm(): lax.psum(jnp.sum(centered * centered, axis=(0, 1, 2, 4)), ('tm', 'space'))  147 us
    ppermute x2, waiting for transfers between devices, passed_along(): return lax.ppermute(shard, axis, pairs)  13.7 us
    dot_general x18, matrix products, causal_conv(): jnp.dot(patch.reshape(frames * rows * columns, 3 * chans), weights[offset...  12.5 us
    slice x5, local copies, waits for them, and re-layouts, causal_conv(): padded[offset_t:offset_t + frames, offset_h:offset_h + rows, shift_w:shif...  8.85 us
    ppermute x2, waiting for transfers between devices, with_halo(): lax.ppermute(lax.slice_in_dim(block, 0, width, axis=dim), axis, backward)  8.79 us
  transfers between devices with their start and end apart: 6, of which 6 were waited for; matrix products, arithmetic and copies ran while one was open for 3% of the time, Pallas kernels for 0%

commit v1 on v0

v1 whole, which is shorter than its diff:
```python
import functools

import jax
import jax.numpy as jnp
from jax import lax
from jax.experimental import pallas as pl
from jax.experimental.pallas import tpu as pltpu
from jax.sharding import PartitionSpec as P

GROUP = 8
EPS = 1e-06
DMA = pltpu.SemaphoreType.DMA

HALO_0 = ((0, 1), (7, 1), (1, 2), (3, 2), (5, 2))
HALO_1 = ((0, 1), (1, 3), (7, 1), (4, 1), (5, 2))
STEPS_0 = ((0, 2, (2,)), (2, 2, (3,)), (4, 4, (4,)))
STEPS_1 = ((0, 2, (1,)), (2, 2, (3,)), (4, 4, (4,)))


def lane_groups(tile):
    lanes = tile.shape[1]
    lane = lax.broadcasted_iota(jnp.int32, tile.shape, 1)
    step = 1
    while step < GROUP:
        ahead = pltpu.roll(tile, lanes - step, 1)
        behind = pltpu.roll(tile, step, 1)
        tile = tile + jnp.where(lane % (2 * step) < step, ahead, behind)
        step *= 2
    return tile


def merged(parts, each):
    total = jnp.sum(parts, 0)
    mean = total * (1.0 / parts.shape[0])
    off = parts - mean
    spread = jnp.sum(off * off, 0) * each
    shifted = pltpu.roll(spread, 2, 0)
    line = lax.broadcasted_iota(jnp.int32, total.shape, 0)
    return jnp.where(line < 2, mean, total + shifted)


def packed(mean, squares):
    half = mean.shape[1] // 2
    line = lax.broadcasted_iota(jnp.int32, (8, half), 0)
    rows = (mean[:, :half], mean[:, half:], squares[:, :half], squares[:, half:])
    tile = jnp.zeros((8, half), jnp.float32)
    for i, row in enumerate(rows):
        tile = jnp.where(line == i, jnp.broadcast_to(row, (8, half)), tile)
    return tile


def affine(tile, count, gain, shift):
    mean = lane_groups(tile) * (1.0 / GROUP)
    off = tile - mean
    inner = pltpu.roll(off * off * count, 2, 0)
    variance = lane_groups(tile + inner) * (1.0 / (GROUP * count))
    mean = jnp.concatenate([mean[0:1], mean[1:2]], 1)
    variance = jnp.concatenate([variance[2:3], variance[3:4]], 1)
    return mean, gain / jnp.sqrt(variance + EPS), shift


def activated(raw, norm):
    mean, scale, shift = norm
    u = (raw.astype(jnp.float32) - mean) * scale + shift
    return u / (1.0 + jnp.exp(-u))


def folded(value):
    cells, chans = value.shape
    return jnp.sum(value.reshape(cells // 8, 8, chans), 0)


def joined(wide, rows, columns, chans):
    wide = wide.reshape(rows, columns, 3 * chans)
    column = lax.broadcasted_iota(jnp.int32, (rows, columns, chans), 1)
    left = jnp.where(column == 0, 0.0, pltpu.roll(wide[:, :, :chans], 1, 1))
    right = jnp.where(
        column == columns - 1, 0.0, pltpu.roll(wide[:, :, 2 * chans :], columns - 1, 1)
    )
    return left + wide[:, :, chans : 2 * chans] + right


def products(field, weight, layer, taps, row, rows):
    columns, chans = field.shape[2:]
    left = [
        field[frame, row + dh : row + dh + rows].reshape(rows * columns, chans)
        for _, frame in taps
        for dh in range(3)
    ]
    right = [weight[layer, dt].reshape(3 * chans, 3 * chans) for dt, _ in taps]
    wide = jnp.dot(
        jnp.concatenate(left, 1),
        jnp.concatenate(right, 0),
        preferred_element_type=jnp.float32,
    )
    return joined(wide, rows, columns, chans)


def kernel(
    frames_all, lines_all,
    features, weights, bias, gain, shift, out,
    raw0, raw1, act0, act1, weight, total, result, space_stats, tm_stats, pivot,
    in_sem, weight_sem, out_sem,
    halo_send, halo_recv, edge_send, edge_recv, far_send, far_recv, stat_send, stat_recv,
):
    t, s = lax.axis_index("tm"), lax.axis_index("space")
    later, above, below = lax.rem(t + 1, frames_all), lax.rem(s + lines_all - 1, lines_all), lax.rem(s + 1, lines_all)
    frames, rows, columns, chans = result.shape
    cells = frames * rows * columns
    first = t == 0
    raws, acts = (raw0, raw1), (act0, act1)

    load = pltpu.make_async_copy(features, raw0.at[pl.ds(2, frames), pl.ds(1, rows)], in_sem)
    load.start()
    loads = []
    for layer in range(2):
        for dw in range(3):
            loads.append(
                pltpu.make_async_copy(
                    weights.at[layer, :, :, dw],
                    weight.at[layer, :, :, :, pl.ds(dw * chans, chans)],
                    weight_sem.at[layer, dw],
                )
            )
            loads[-1].start()

    barrier = pltpu.get_barrier_semaphore()

    @pl.loop(1, lines_all)
    def _(j):
        pl.semaphore_signal(barrier, inc=1, device_id=(t, lax.rem(s + j, lines_all)), device_id_type=pl.DeviceIdType.MESH)

    @pl.loop(1, frames_all)
    def _(j):
        pl.semaphore_signal(barrier, inc=1, device_id=(lax.rem(t + j, frames_all), s), device_id_type=pl.DeviceIdType.MESH)

    def remote(source, target, send, recv, device):
        return pltpu.make_async_remote_copy(
            src_ref=source, dst_ref=target, send_sem=send, recv_sem=recv,
            device_id=device, device_id_type=pl.DeviceIdType.MESH,
        )

    def halo(layer, order, k):
        row, count = order[k]
        raw = raws[layer]
        return remote(
            raw.at[pl.ds(2, 2), pl.ds(1 + row, count)],
            raw.at[pl.ds(0, 2), pl.ds(1 + row, count)],
            halo_send.at[layer, k], halo_recv.at[layer, k], (later, s),
        )

    def edge(layer, frame, side, sems):
        raw = raws[layer]
        source, target = ((1, rows + 1), (rows, 0))[side]
        return remote(
            raw.at[pl.ds(frame, 2), source], raw.at[pl.ds(frame, 2), target],
            sems[0].at[layer, side], sems[1].at[layer, side], (t, (above, below)[side]),
        )

    def own_edge(layer, side):
        return edge(layer, 2, side, (edge_send, edge_recv))

    def far_edge(layer, side):
        return edge(layer, 0, side, (far_send, far_recv))

    def spread_start(layer, stage):
        buffer = (space_stats, tm_stats)[stage]
        number = buffer.shape[1]

        @pl.loop(1, number)
        def _(j):
            device = ((t, lax.rem(s + j, lines_all)), (lax.rem(t + j, frames_all), s))[stage]
            remote(
                buffer.at[layer, 0], buffer.at[layer, j],
                stat_send.at[layer, stage], stat_recv.at[layer, stage], device,
            ).start()

    def spread_wait(layer, stage, sems):
        buffer = (space_stats, tm_stats)[stage]
        rest = buffer.at[layer, pl.ds(1, buffer.shape[1] - 1)]
        pltpu.make_async_copy(rest, rest, sems.at[layer, stage]).wait()

    def normalize(layer, norm, frame, row, count):
        raw, act = raws[layer], acts[layer]
        value = raw[frame, pl.ds(row, count)]
        if isinstance(frame, int) and frame < 2:
            value = jnp.where(first, raw[2, pl.ds(row, count)], value)
        value = activated(value, norm)
        if isinstance(row, int) and row in (0, rows + 1):
            outside = s == (0 if row == 0 else lines_all - 1)
            value = jnp.where(outside, 0.0, value)
        act[frame, pl.ds(row, count)] = value.astype(jnp.bfloat16)

    def own_part(layer, norm):
        for side in range(2):
            own_edge(layer, side).wait_recv()
        for frame in (2, 3):
            for row in (0, rows + 1):
                normalize(layer, norm, frame, row, 1)

            @pl.loop(0, rows)
            def _(row):
                normalize(layer, norm, frame, row + 1, 1)

        if layer == 0:
            for dw in range(3):
                loads[dw].wait()
        else:
            for dw in range(3):
                loads[3 + dw].wait()
        act = acts[layer]
        total[0] = products(act, weight, layer, ((2, 2),), 0, rows) + bias[layer : layer + 1]
        total[1] = products(act, weight, layer, ((1, 2), (2, 3)), 0, rows) + bias[layer : layer + 1]

    def halo_part(layer, norm, steps, order, finish):
        act = acts[layer]
        done = 0
        ready = -1
        for k, (row, count, need) in enumerate(steps):
            for c in range(done, need[-1] + 1):
                if order[c][0] not in (0, rows - 1):
                    halo(layer, order, c).wait_recv()
            done = need[-1] + 1
            if k == 0:
                far_edge(layer, 1).wait_recv()
                for frame in (0, 1):
                    normalize(layer, norm, frame, 0, 1)
            if k == len(steps) - 1:
                far_edge(layer, 0).wait_recv()
                for frame in (0, 1):
                    normalize(layer, norm, frame, rows + 1, 1)
            upto = min(row + count, rows - 1)
            for frame in (0, 1):
                normalize(layer, norm, frame, ready + 2, upto - ready)
            ready = upto
            values = (
                products(act, weight, layer, ((0, 0), (1, 1)), row, count),
                products(act, weight, layer, ((0, 1),), row, count),
            )
            finish(k, row, count, values)

    load.wait()

    def lines(f):
        return lax.fori_loop(
            0, frames * rows,
            lambda i, carry: carry + folded(f(raw0[2 + i // rows, 1 + i % rows].astype(jnp.float32))),
            jnp.zeros((8, chans), jnp.float32),
        )

    mean = jnp.sum(lines(lambda v: v), 0, keepdims=True) * (1.0 / cells)
    squares = jnp.sum(lines(lambda v: (v - mean) * (v - mean)), 0, keepdims=True)
    space_stats[0, 0] = packed(mean, squares)

    pl.semaphore_wait(barrier, lines_all + frames_all - 2)

    halo(0, HALO_0, 0).start()
    halo(0, HALO_0, 1).start()
    spread_start(0, 0)
    for side in range(2):
        own_edge(0, side).start()
    for k in range(2, len(HALO_0)):
        halo(0, HALO_0, k).start()

    def statistics(layer, order, between):
        spread_wait(layer, 0, stat_recv)
        tm_stats[layer, 0] = merged(space_stats[layer], float(cells))
        spread_start(layer, 1)
        between()
        spread_wait(layer, 1, stat_recv)
        tile = merged(tm_stats[layer], float(cells * lines_all))
        return affine(
            tile, float(cells * lines_all * frames_all),
            gain[layer : layer + 1], shift[layer : layer + 1],
        )

    def forward_edges(layer, order):
        for k, (row, _) in enumerate(order):
            if row in (0, rows - 1):
                halo(layer, order, k).wait_recv()
                far_edge(layer, 0 if row == 0 else 1).start()

    norm0 = statistics(0, HALO_0, lambda: forward_edges(0, HALO_0))
    own_part(0, norm0)

    sums = [jnp.zeros((8, chans), jnp.float32), jnp.zeros((8, chans), jnp.float32)]

    def finish_0(k, row, count, values):
        chunk = []
        for frame in range(2):
            value = (total[frame, row : row + count] + values[frame]).astype(jnp.bfloat16)
            raw1[2 + frame, 1 + row : 1 + row + count] = value
            chunk.append(value.astype(jnp.float32).reshape(count * columns, chans))
        if k == 0:
            pivot[...] = jnp.sum(folded(chunk[0]) + folded(chunk[1]), 0, keepdims=True) * (
                1.0 / (2 * count * columns)
            )
        base = pivot[...]
        for value in chunk:
            off = value - base
            sums[0] = sums[0] + folded(off)
            sums[1] = sums[1] + folded(off * off)
        if k == 0:
            own_edge(1, 0).start()
        if k == len(STEPS_0) - 2:
            for c in range(len(HALO_0)):
                halo(0, HALO_0, c).wait_send()
            halo(1, HALO_1, 0).start()
            halo(1, HALO_1, 1).start()
        if k == len(STEPS_0) - 1:
            own_edge(1, 1).start()
            for c in range(2, len(HALO_1)):
                halo(1, HALO_1, c).start()

    halo_part(0, norm0, STEPS_0, HALO_0, finish_0)

    off_mean = jnp.sum(sums[0], 0, keepdims=True) * (1.0 / cells)
    off_squares = jnp.sum(sums[1], 0, keepdims=True)
    space_stats[1, 0] = packed(pivot[...] + off_mean, off_squares - off_mean * off_mean * cells)
    spread_start(1, 0)
    norm1 = statistics(1, HALO_1, lambda: forward_edges(1, HALO_1))
    own_part(1, norm1)

    def store(k, row, count):
        return pltpu.make_async_copy(
            result.at[:, pl.ds(row, count)], out.at[:, pl.ds(row, count)], out_sem.at[k]
        )

    def finish_1(k, row, count, values):
        for frame in range(2):
            value = total[frame, row : row + count] + values[frame]
            value = value + raw0[2 + frame, 1 + row : 1 + row + count].astype(jnp.float32)
            result[frame, row : row + count] = value.astype(jnp.bfloat16)
        store(k, row, count).start()

    halo_part(1, norm1, STEPS_1, HALO_1, finish_1)

    for layer in range(2):
        for stage in range(2):
            spread_wait(layer, stage, stat_send)
        for side in range(2):
            own_edge(layer, side).wait_send()
            far_edge(layer, side).wait_send()
    for k in range(len(HALO_1)):
        halo(1, HALO_1, k).wait_send()
    for k, (row, count, _) in enumerate(STEPS_1):
        store(k, row, count).wait()


def shards(features, weights, bias, gain, shift):
    frames, rows, columns, chans = features.shape
    frames_all, lines_all = lax.axis_size("tm"), lax.axis_size("space")
    field = pltpu.VMEM((frames + 2, rows + 2, columns, chans), jnp.bfloat16)
    anywhere, here = pl.BlockSpec(memory_space=pl.ANY), pl.BlockSpec(memory_space=pltpu.VMEM)
    return pl.pallas_call(
        functools.partial(kernel, frames_all, lines_all),
        out_shape=jax.ShapeDtypeStruct(features.shape, features.dtype),
        in_specs=[anywhere, anywhere, here, here, here],
        out_specs=anywhere,
        scratch_shapes=[
            field, field, field, field,
            pltpu.VMEM((2, 3, 3, chans, 3 * chans), jnp.bfloat16),
            pltpu.VMEM((frames, rows, columns, chans), jnp.float32),
            pltpu.VMEM((frames, rows, columns, chans), jnp.bfloat16),
            pltpu.VMEM((2, lines_all, 8, 128), jnp.float32),
            pltpu.VMEM((2, frames_all, 8, 128), jnp.float32),
            pltpu.VMEM((1, chans), jnp.float32),
            DMA, DMA((2, 3)), DMA((len(STEPS_1),)),
            DMA((2, len(HALO_0))), DMA((2, len(HALO_0))),
            DMA((2, 2)), DMA((2, 2)), DMA((2, 2)), DMA((2, 2)),
            DMA((2, 2)), DMA((2, 2)),
        ],
        compiler_params=pltpu.CompilerParams(
            collective_id=0, has_side_effects=True, vmem_limit_bytes=56 * 2**20
        ),
        cost_estimate=pl.CostEstimate(
            flops=4 * frames * rows * columns * 27 * chans * chans,
            bytes_accessed=2 * features.size * 2 + weights.size * 2,
            transcendentals=0,
        ),
    )(features, weights, bias, gain, shift)


def solution(mesh):
    placed = (P("tm", "space", None, None), P(), P(), P(), P())
    return jax.shard_map(
        shards, mesh=mesh, in_specs=placed, out_specs=P("tm", "space", None, None), check_vma=False
    )
```

time: 402 us -> 61.2 us (0.15)
  blocking collectives: 306 us -> 0 us
  Pallas kernels: 0 us -> 59.1 us
  local copies, waits for them, and re-layouts: 25.8 us -> 1.97 us
  waiting for transfers between devices: 22.9 us -> 0 us
  starting transfers between devices: 19.5 us -> 0 us
  matrix products: 12.5 us -> 0 us
  other arithmetic: 11.3 us -> 0 us
    psum x4 -> x0, blocking collectives: 306 us -> none  [the longest x2 160 us: group_norm(): totals = lax.psum(jnp.sum(grouped, axis=(0, 1, 2, 4)), ('tm', 'space'))]
    pallas_call x0 -> x1, Pallas kernels: none -> 59.1 us  [shards(): pl.pallas_call(functools.partial(kernel, frames_all, lines_all), out_shap...]
    ppermute x6 -> x0, waiting for transfers between devices: 22.9 us -> none  [the longest x2 13.7 us: passed_along(): return lax.ppermute(shard, axis, pairs)]
    ppermute x6 -> x0, starting transfers between devices: 19.5 us -> none  [the longest x2 7.98 us: with_halo(): lax.ppermute(lax.slice_in_dim(block, block.shape[dim] - width, None, axis...]
    slice x11 -> x0, local copies, waits for them, and re-layouts: 15.8 us -> none  [the longest x5 8.85 us: causal_conv(): padded[offset_t:offset_t + frames, offset_h:offset_h + rows, shift_w:shif...]
    dot_general x18 -> x0, matrix products: 12.5 us -> none  [causal_conv(): jnp.dot(patch.reshape(frames * rows * columns, 3 * chans), weights[offset...]
    squeeze x1 -> x0, local copies, waits for them, and re-layouts: 6.8 us -> none  [shards(): conv_weights[1]]
    concatenate x18 -> x0, other arithmetic: 4.65 us -> none  [the longest x14 2.64 us: causal_conv(): jnp.concatenate([padded[offset_t:offset_t + frames, offset_h:offset_h + r...]
  transfers between devices with their start and end apart: 6 -> 0, of which waited for: 6 -> 0; matrix products, arithmetic and copies ran while one was open for 3% -> 0% of each run, Pallas kernels for 0% -> 0%
where the time goes in v1:
time: 61.2 us; the launch traced here: 61 us
  Pallas kernels  59.1 us (97%)
  local copies, waits for them, and re-layouts  1.97 us (3%)
    pallas_call x1, Pallas kernels, shards(): pl.pallas_call(functools.partial(kernel, frames_all, lines_all), out_shap...  59.1 us
    unnamed x1, local copies, waits for them, and re-layouts  1.97 us

profile of v1, /device:TPU:1, one launch (start us, length us, event | category | flops | bytes accessed | tf_op | source)
XLA Modules:
  0.0 61.0 jit_solution(15366393475304530031)
XLA Ops:
  0.0 59.1 %shard_map.55 = bf16[2,8,80,256]{3,2,1,0:T(8,128)(2,1)} custom-call(bf16[2,8,80,256]{3,2,1,0:T(8,128)(2,1)} %features.1, bf16[2,3,3,3,256,256]{5,4,3,2,1,0:T(8,128)(2,1)} %weights.1, f32[2,256]{1,0:T(2,128)} %bias.1, f32[2,256]{1,0:T(2,128)} %gain.1, f32[2,256]{1,0:T(2,128)} %shift.1), custom_call_target="tpu_custom_call" | custom-call | flops 9059696640 | bytes 8388608 | tf_op jit(solution)/shard_map/pallas_call | solution.py:355
  59.1 2.0 %copy.7 = bf16[2,8,80,256]{3,2,1,0:T(8,128)(2,1)} copy(bf16[2,8,80,256]{3,2,1,0:T(8,128)(2,1)} %shard_map.55) | data formatting | bytes 1310720

commit v2 on v1

--- a/solution.py
+++ b/solution.py
@@ -11,10 +11,11 @@
 EPS = 1e-06
 DMA = pltpu.SemaphoreType.DMA
 
-HALO_0 = ((0, 1), (7, 1), (1, 2), (3, 2), (5, 2))
+HALO_0 = ((0, 1), (7, 1), (1, 1), (2, 1), (3, 2), (5, 2))
 HALO_1 = ((0, 1), (1, 3), (7, 1), (4, 1), (5, 2))
-STEPS_0 = ((0, 2, (2,)), (2, 2, (3,)), (4, 4, (4,)))
-STEPS_1 = ((0, 2, (1,)), (2, 2, (3,)), (4, 4, (4,)))
+AHEAD = (3, 2)
+STEPS_0 = ((0, 2, 3), (2, 2, 4), (4, 4, 5))
+STEPS_1 = ((0, 2, 1), (2, 2, 3), (4, 4, 4))
 
 
 def lane_groups(tile):
@@ -99,16 +100,26 @@
 def kernel(
     frames_all, lines_all,
     features, weights, bias, gain, shift, out,
-    raw0, raw1, act0, act1, weight, total, result, space_stats, tm_stats, pivot,
-    in_sem, weight_sem, out_sem,
+    raw0, raw1, act0, act1, weight, total, space_stats, tm_stats, pivot,
+    in_sem, weight_sem,
     halo_send, halo_recv, edge_send, edge_recv, far_send, far_recv, stat_send, stat_recv,
 ):
     t, s = lax.axis_index("tm"), lax.axis_index("space")
     later, above, below = lax.rem(t + 1, frames_all), lax.rem(s + lines_all - 1, lines_all), lax.rem(s + 1, lines_all)
-    frames, rows, columns, chans = result.shape
+    frames, rows, columns, chans = out.shape
     cells = frames * rows * columns
     first = t == 0
     raws, acts = (raw0, raw1), (act0, act1)
+
+    barrier = pltpu.get_barrier_semaphore()
+
+    @pl.loop(1, lines_all)
+    def _(j):
+        pl.semaphore_signal(barrier, inc=1, device_id=(t, lax.rem(s + j, lines_all)), device_id_type=pl.DeviceIdType.MESH)
+
+    @pl.loop(1, frames_all)
+    def _(j):
+        pl.semaphore_signal(barrier, inc=1, device_id=(lax.rem(t + j, frames_all), s), device_id_type=pl.DeviceIdType.MESH)
 
     load = pltpu.make_async_copy(features, raw0.at[pl.ds(2, frames), pl.ds(1, rows)], in_sem)
     load.start()
@@ -124,16 +135,6 @@
             )
             loads[-1].start()
 
-    barrier = pltpu.get_barrier_semaphore()
-
-    @pl.loop(1, lines_all)
-    def _(j):
-        pl.semaphore_signal(barrier, inc=1, device_id=(t, lax.rem(s + j, lines_all)), device_id_type=pl.DeviceIdType.MESH)
-
-    @pl.loop(1, frames_all)
-    def _(j):
-        pl.semaphore_signal(barrier, inc=1, device_id=(lax.rem(t + j, frames_all), s), device_id_type=pl.DeviceIdType.MESH)
-
     def remote(source, target, send, recv, device):
         return pltpu.make_async_remote_copy(
             src_ref=source, dst_ref=target, send_sem=send, recv_sem=recv,
@@ -167,8 +168,9 @@
         buffer = (space_stats, tm_stats)[stage]
         number = buffer.shape[1]
 
-        @pl.loop(1, number)
-        def _(j):
+        @pl.loop(0, number - 1)
+        def _(i):
+            j = lax.rem(i + number // 3, number - 1) + 1
             device = ((t, lax.rem(s + j, lines_all)), (lax.rem(t + j, frames_all), s))[stage]
             remote(
                 buffer.at[layer, 0], buffer.at[layer, j],
@@ -217,10 +219,10 @@
         done = 0
         ready = -1
         for k, (row, count, need) in enumerate(steps):
-            for c in range(done, need[-1] + 1):
+            for c in range(done, need + 1):
                 if order[c][0] not in (0, rows - 1):
                     halo(layer, order, c).wait_recv()
-            done = need[-1] + 1
+            done = need + 1
             if k == 0:
                 far_edge(layer, 1).wait_recv()
                 for frame in (0, 1):
@@ -254,18 +256,18 @@
 
     pl.semaphore_wait(barrier, lines_all + frames_all - 2)
 
-    halo(0, HALO_0, 0).start()
-    halo(0, HALO_0, 1).start()
+    for k in range(AHEAD[0]):
+        halo(0, HALO_0, k).start()
     spread_start(0, 0)
     for side in range(2):
         own_edge(0, side).start()
-    for k in range(2, len(HALO_0)):
-        halo(0, HALO_0, k).start()
 
     def statistics(layer, order, between):
         spread_wait(layer, 0, stat_recv)
         tm_stats[layer, 0] = merged(space_stats[layer], float(cells))
         spread_start(layer, 1)
+        for k in range(AHEAD[layer], len(order)):
+            halo(layer, order, k).start()
         between()
         spread_wait(layer, 1, stat_recv)
         tile = merged(tm_stats[layer], float(cells * lines_all))
@@ -303,13 +305,7 @@
         if k == 0:
             own_edge(1, 0).start()
         if k == len(STEPS_0) - 2:
-            for c in range(len(HALO_0)):
-                halo(0, HALO_0, c).wait_send()
-            halo(1, HALO_1, 0).start()
-            halo(1, HALO_1, 1).start()
-        if k == len(STEPS_0) - 1:
-            own_edge(1, 1).start()
-            for c in range(2, len(HALO_1)):
+            for c in range(AHEAD[1]):
                 halo(1, HALO_1, c).start()
 
     halo_part(0, norm0, STEPS_0, HALO_0, finish_0)
@@ -318,20 +314,15 @@
     off_squares = jnp.sum(sums[1], 0, keepdims=True)
     space_stats[1, 0] = packed(pivot[...] + off_mean, off_squares - off_mean * off_mean * cells)
     spread_start(1, 0)
+    own_edge(1, 1).start()
     norm1 = statistics(1, HALO_1, lambda: forward_edges(1, HALO_1))
     own_part(1, norm1)
-
-    def store(k, row, count):
-        return pltpu.make_async_copy(
-            result.at[:, pl.ds(row, count)], out.at[:, pl.ds(row, count)], out_sem.at[k]
-        )
 
     def finish_1(k, row, count, values):
         for frame in range(2):
             value = total[frame, row : row + count] + values[frame]
             value = value + raw0[2 + frame, 1 + row : 1 + row + count].astype(jnp.float32)
-            result[frame, row : row + count] = value.astype(jnp.bfloat16)
-        store(k, row, count).start()
+            out[frame, row : row + count] = value.astype(jnp.bfloat16)
 
     halo_part(1, norm1, STEPS_1, HALO_1, finish_1)
 
@@ -341,32 +332,31 @@
         for side in range(2):
             own_edge(layer, side).wait_send()
             far_edge(layer, side).wait_send()
+    for k in range(len(HALO_0)):
+        halo(0, HALO_0, k).wait_send()
     for k in range(len(HALO_1)):
         halo(1, HALO_1, k).wait_send()
-    for k, (row, count, _) in enumerate(STEPS_1):
-        store(k, row, count).wait()
 
 
 def shards(features, weights, bias, gain, shift):
     frames, rows, columns, chans = features.shape
     frames_all, lines_all = lax.axis_size("tm"), lax.axis_size("space")
     field = pltpu.VMEM((frames + 2, rows + 2, columns, chans), jnp.bfloat16)
-    anywhere, here = pl.BlockSpec(memory_space=pl.ANY), pl.BlockSpec(memory_space=pltpu.VMEM)
+    there, here = pl.BlockSpec(memory_space=pltpu.HBM), pl.BlockSpec(memory_space=pltpu.VMEM)
     return pl.pallas_call(
         functools.partial(kernel, frames_all, lines_all),
-        out_shape=jax.ShapeDtypeStruct(features.shape, features.dtype),
-        in_specs=[anywhere, anywhere, here, here, here],
-        out_specs=anywhere,
+        out_shape=pltpu.VMEM(features.shape, features.dtype),
+        in_specs=[there, there, here, here, here],
+        out_specs=here,
         scratch_shapes=[
             field, field, field, field,
             pltpu.VMEM((2, 3, 3, chans, 3 * chans), jnp.bfloat16),
             pltpu.VMEM((frames, rows, columns, chans), jnp.float32),
-            pltpu.VMEM((frames, rows, columns, chans), jnp.bfloat16),
             pltpu.VMEM((2, lines_all, 8, 128), jnp.float32),
             pltpu.VMEM((2, frames_all, 8, 128), jnp.float32),
             pltpu.VMEM((1, chans), jnp.float32),
-            DMA, DMA((2, 3)), DMA((len(STEPS_1),)),
-            DMA((2, len(HALO_0))), DMA((2, len(HALO_0))),
+            DMA, DMA((2, 3)),
+            DMA((2, 8)), DMA((2, 8)),
             DMA((2, 2)), DMA((2, 2)), DMA((2, 2)), DMA((2, 2)),
             DMA((2, 2)), DMA((2, 2)),
         ],

time: 61.2 us -> 49 us (0.80)
  Pallas kernels: 59.1 us -> 48.1 us
  local copies, waits for them, and re-layouts: 1.97 us -> 0.84 us
    pallas_call x1, Pallas kernels: 59.1 us -> 48.1 us  [shards(): pl.pallas_call(functools.partial(kernel, frames_all, lines_all), out_shap...]
    unnamed x1, local copies, waits for them, and re-layouts: 1.97 us -> 0.84 us
where the time goes in v2:
time: 49 us; the launch traced here: 48.9 us
  Pallas kernels  48.1 us (98%)
  local copies, waits for them, and re-layouts  0.84 us (2%)
    pallas_call x1, Pallas kernels, shards(): pl.pallas_call(functools.partial(kernel, frames_all, lines_all), out_shap...  48.1 us

profile of v2, /device:TPU:1, one launch (start us, length us, event | category | flops | bytes accessed | tf_op | source)
XLA Modules:
  0.0 48.9 jit_solution(8818904017561620076)
XLA Ops:
  0.0 48.1 %shard_map.55 = bf16[2,8,80,256]{3,2,1,0:T(8,128)(2,1)S(1)} custom-call(bf16[2,8,80,256]{3,2,1,0:T(8,128)(2,1)} %features.1, bf16[2,3,3,3,256,256]{5,4,3,2,1,0:T(8,128)(2,1)} %weights.1, f32[2,256]{1,0:T(2,128)} %bias.1, f32[2,256]{1,0:T(2,128)} %gain.1, f32[2,256]{1,0:T(2,128)} %shift.1), custom_call_target="tpu_custom_call" | custom-call | flops 9059696640 | bytes 8388608 | tf_op jit(solution)/shard_map/pallas_call | solution.py:346
  48.1 0.8 %copy.7 = bf16[2,8,80,256]{3,2,1,0:T(8,128)(2,1)} copy(bf16[2,8,80,256]{3,2,1,0:T(8,128)(2,1)S(1)} %shard_map.55) | data formatting | bytes 1310720

commit v3 on v2

--- a/solution.py
+++ b/solution.py
@@ -11,11 +11,11 @@
 EPS = 1e-06
 DMA = pltpu.SemaphoreType.DMA
 
-HALO_0 = ((0, 1), (7, 1), (1, 1), (2, 1), (3, 2), (5, 2))
-HALO_1 = ((0, 1), (1, 3), (7, 1), (4, 1), (5, 2))
-AHEAD = (3, 2)
-STEPS_0 = ((0, 2, 3), (2, 2, 4), (4, 4, 5))
-STEPS_1 = ((0, 2, 1), (2, 2, 3), (4, 4, 4))
+HALO_0 = ((0, 1), (7, 1), (1, 1), (2, 2), (4, 2), (6, 1))
+HALO_1 = ((0, 1), (1, 2), (3, 1), (4, 1), (7, 1), (5, 1), (6, 1))
+AHEAD = (3, 3)
+STEPS_0 = ((0, 3, 3), (3, 2, 4), (5, 3, 5))
+STEPS_1 = ((0, 3, 2), (3, 2, 5), (5, 3, 6))
 
 
 def lane_groups(tile):
@@ -57,13 +57,13 @@
     variance = lane_groups(tile + inner) * (1.0 / (GROUP * count))
     mean = jnp.concatenate([mean[0:1], mean[1:2]], 1)
     variance = jnp.concatenate([variance[2:3], variance[3:4]], 1)
-    return mean, gain / jnp.sqrt(variance + EPS), shift
+    return mean, 0.5 * gain / jnp.sqrt(variance + EPS), 0.5 * shift
 
 
 def activated(raw, norm):
     mean, scale, shift = norm
-    u = (raw.astype(jnp.float32) - mean) * scale + shift
-    return u / (1.0 + jnp.exp(-u))
+    half = (raw.astype(jnp.float32) - mean) * scale + shift
+    return half + half * jnp.tanh(half)
 
 
 def folded(value):
@@ -173,13 +173,13 @@
             j = lax.rem(i + number // 3, number - 1) + 1
             device = ((t, lax.rem(s + j, lines_all)), (lax.rem(t + j, frames_all), s))[stage]
             remote(
-                buffer.at[layer, 0], buffer.at[layer, j],
+                buffer.at[layer, 0, pl.ds(0, 4)], buffer.at[layer, j, pl.ds(0, 4)],
                 stat_send.at[layer, stage], stat_recv.at[layer, stage], device,
             ).start()
 
     def spread_wait(layer, stage, sems):
         buffer = (space_stats, tm_stats)[stage]
-        rest = buffer.at[layer, pl.ds(1, buffer.shape[1] - 1)]
+        rest = buffer.at[layer, pl.ds(1, buffer.shape[1] - 1), pl.ds(0, 4)]
         pltpu.make_async_copy(rest, rest, sems.at[layer, stage]).wait()
 
     def normalize(layer, norm, frame, row, count):
@@ -196,23 +196,26 @@
     def own_part(layer, norm):
         for side in range(2):
             own_edge(layer, side).wait_recv()
+        for dw in range(3):
+            loads[3 * layer + dw].wait()
+        act = acts[layer]
+        half = rows // 2
+        added = bias[layer : layer + 1]
         for frame in (2, 3):
-            for row in (0, rows + 1):
-                normalize(layer, norm, frame, row, 1)
-
-            @pl.loop(0, rows)
+            normalize(layer, norm, frame, 0, 1)
+
+            @pl.loop(0, half + 1)
             def _(row):
                 normalize(layer, norm, frame, row + 1, 1)
 
-        if layer == 0:
-            for dw in range(3):
-                loads[dw].wait()
-        else:
-            for dw in range(3):
-                loads[3 + dw].wait()
-        act = acts[layer]
-        total[0] = products(act, weight, layer, ((2, 2),), 0, rows) + bias[layer : layer + 1]
-        total[1] = products(act, weight, layer, ((1, 2), (2, 3)), 0, rows) + bias[layer : layer + 1]
+        total[0, :half] = products(act, weight, layer, ((2, 2),), 0, half) + added
+        normalize(layer, norm, 2, half + 2, half - 1)
+        normalize(layer, norm, 2, rows + 1, 1)
+        total[1, :half] = products(act, weight, layer, ((1, 2), (2, 3)), 0, half) + added
+        normalize(layer, norm, 3, half + 2, half - 1)
+        normalize(layer, norm, 3, rows + 1, 1)
+        total[0, half:] = products(act, weight, layer, ((2, 2),), half, half) + added
+        total[1, half:] = products(act, weight, layer, ((1, 2), (2, 3)), half, half) + added
 
     def halo_part(layer, norm, steps, order, finish):
         act = acts[layer]
@@ -243,15 +246,20 @@
 
     load.wait()
 
-    def lines(f):
-        return lax.fori_loop(
-            0, frames * rows,
-            lambda i, carry: carry + folded(f(raw0[2 + i // rows, 1 + i % rows].astype(jnp.float32))),
-            jnp.zeros((8, chans), jnp.float32),
-        )
-
-    mean = jnp.sum(lines(lambda v: v), 0, keepdims=True) * (1.0 / cells)
-    squares = jnp.sum(lines(lambda v: (v - mean) * (v - mean)), 0, keepdims=True)
+    base = jnp.sum(folded(raw0[2, 1].astype(jnp.float32)), 0, keepdims=True) * (1.0 / columns)
+
+    def line(i, carry):
+        sums = list(carry)
+        for frame in range(frames):
+            off = raw0[2 + frame, 1 + i].astype(jnp.float32) - base
+            sums[0] = sums[0] + folded(off)
+            sums[1] = sums[1] + folded(off * off)
+        return tuple(sums)
+
+    empty = jnp.zeros((8, chans), jnp.float32)
+    sums = [jnp.sum(part, 0, keepdims=True) for part in lax.fori_loop(0, rows, line, (empty, empty))]
+    off_mean = sums[0] * (1.0 / cells)
+    mean, squares = base + off_mean, sums[1] - off_mean * off_mean * cells
     space_stats[0, 0] = packed(mean, squares)
 
     pl.semaphore_wait(barrier, lines_all + frames_all - 2)
@@ -304,8 +312,9 @@
             sums[1] = sums[1] + folded(off * off)
         if k == 0:
             own_edge(1, 0).start()
-        if k == len(STEPS_0) - 2:
-            for c in range(AHEAD[1]):
+        for c in range(AHEAD[1]):
+            last = sum(HALO_1[c]) - 1
+            if row <= last < row + count:
                 halo(1, HALO_1, c).start()
 
     halo_part(0, norm0, STEPS_0, HALO_0, finish_0)

time: 49 us -> 48.4 us (0.988)
  Pallas kernels: 48.1 us -> 47.5 us
    pallas_call x1, Pallas kernels: 48.1 us -> 47.5 us  [shards(): pl.pallas_call(functools.partial(kernel, frames_all, lines_all), out_shap...]
where the time goes in v3:
time: 48.4 us; the launch traced here: 48.3 us
  Pallas kernels  47.5 us (98%)
  local copies, waits for them, and re-layouts  0.84 us (2%)
    pallas_call x1, Pallas kernels, shards(): pl.pallas_call(functools.partial(kernel, frames_all, lines_all), out_shap...  47.5 us

profile of v3, /device:TPU:1, one launch (start us, length us, event | category | flops | bytes accessed | tf_op | source)
XLA Modules:
  0.0 48.3 jit_solution(3216809084041656882)
XLA Ops:
  0.0 47.5 %shard_map.55 = bf16[2,8,80,256]{3,2,1,0:T(8,128)(2,1)S(1)} custom-call(bf16[2,8,80,256]{3,2,1,0:T(8,128)(2,1)} %features.1, bf16[2,3,3,3,256,256]{5,4,3,2,1,0:T(8,128)(2,1)} %weights.1, f32[2,256]{1,0:T(2,128)} %bias.1, f32[2,256]{1,0:T(2,128)} %gain.1, f32[2,256]{1,0:T(2,128)} %shift.1), custom_call_target="tpu_custom_call" | custom-call | flops 9059696640 | bytes 8388608 | tf_op jit(solution)/shard_map/pallas_call | solution.py:355
  47.5 0.8 %copy.7 = bf16[2,8,80,256]{3,2,1,0:T(8,128)(2,1)} copy(bf16[2,8,80,256]{3,2,1,0:T(8,128)(2,1)S(1)} %shard_map.55) | data formatting | bytes 1310720

commit v4 on v3

--- a/solution.py
+++ b/solution.py
@@ -13,7 +13,7 @@
 
 HALO_0 = ((0, 1), (7, 1), (1, 1), (2, 2), (4, 2), (6, 1))
 HALO_1 = ((0, 1), (1, 2), (3, 1), (4, 1), (7, 1), (5, 1), (6, 1))
-AHEAD = (3, 3)
+AHEAD = (3, 4)
 STEPS_0 = ((0, 3, 3), (3, 2, 4), (5, 3, 5))
 STEPS_1 = ((0, 3, 2), (3, 2, 5), (5, 3, 6))
 

time: 48.4 us -> 47.1 us (0.973)
  Pallas kernels: 47.5 us -> 46.2 us
    pallas_call x1, Pallas kernels: 47.5 us -> 46.2 us  [shards(): pl.pallas_call(functools.partial(kernel, frames_all, lines_all), out_shap...]
where the time goes in v4:
time: 47.1 us; the launch traced here: 47 us
  Pallas kernels  46.2 us (98%)
  local copies, waits for them, and re-layouts  0.84 us (2%)
    pallas_call x1, Pallas kernels, shards(): pl.pallas_call(functools.partial(kernel, frames_all, lines_all), out_shap...  46.2 us

profile of v4, /device:TPU:1, one launch (start us, length us, event | category | flops | bytes accessed | tf_op | source)
XLA Modules:
  0.0 47.0 jit_solution(6275590940534482609)
XLA Ops:
  0.0 46.2 %shard_map.55 = bf16[2,8,80,256]{3,2,1,0:T(8,128)(2,1)S(1)} custom-call(bf16[2,8,80,256]{3,2,1,0:T(8,128)(2,1)} %features.1, bf16[2,3,3,3,256,256]{5,4,3,2,1,0:T(8,128)(2,1)} %weights.1, f32[2,256]{1,0:T(2,128)} %bias.1, f32[2,256]{1,0:T(2,128)} %gain.1, f32[2,256]{1,0:T(2,128)} %shift.1), custom_call_target="tpu_custom_call" | custom-call | flops 9059696640 | bytes 8388608 | tf_op jit(solution)/shard_map/pallas_call | solution.py:355
  46.2 0.8 %copy.7 = bf16[2,8,80,256]{3,2,1,0:T(8,128)(2,1)} copy(bf16[2,8,80,256]{3,2,1,0:T(8,128)(2,1)S(1)} %shard_map.55) | data formatting | bytes 1310720

commit v5 on v4

--- a/solution.py
+++ b/solution.py
@@ -214,13 +214,19 @@
         total[1, :half] = products(act, weight, layer, ((1, 2), (2, 3)), 0, half) + added
         normalize(layer, norm, 3, half + 2, half - 1)
         normalize(layer, norm, 3, rows + 1, 1)
+        if layer == 1:
+            for c in (1, 2):
+                halo(1, HALO_1, c).wait_recv()
         total[0, half:] = products(act, weight, layer, ((2, 2),), half, half) + added
+        if layer == 1:
+            normalize(layer, norm, 0, 1, 4)
         total[1, half:] = products(act, weight, layer, ((1, 2), (2, 3)), half, half) + added
+        if layer == 1:
+            normalize(layer, norm, 1, 1, 4)
 
     def halo_part(layer, norm, steps, order, finish):
         act = acts[layer]
-        done = 0
-        ready = -1
+        done, ready = ((0, -1), (3, 3))[layer]
         for k, (row, count, need) in enumerate(steps):
             for c in range(done, need + 1):
                 if order[c][0] not in (0, rows - 1):
@@ -235,8 +241,9 @@
                 for frame in (0, 1):
                     normalize(layer, norm, frame, rows + 1, 1)
             upto = min(row + count, rows - 1)
-            for frame in (0, 1):
-                normalize(layer, norm, frame, ready + 2, upto - ready)
+            if upto > ready:
+                for frame in (0, 1):
+                    normalize(layer, norm, frame, ready + 2, upto - ready)
             ready = upto
             values = (
                 products(act, weight, layer, ((0, 0), (1, 1)), row, count),

time: 47.1 us -> 47.7 us (1.013)
  Pallas kernels: 46.2 us -> 46.7 us
    pallas_call x1, Pallas kernels: 46.2 us -> 46.7 us  [shards(): pl.pallas_call(functools.partial(kernel, frames_all, lines_all), out_shap...]
where the time goes in v5:
time: 47.7 us; the launch traced here: 47.6 us
  Pallas kernels  46.7 us (98%)
  local copies, waits for them, and re-layouts  0.84 us (2%)
    pallas_call x1, Pallas kernels, shards(): pl.pallas_call(functools.partial(kernel, frames_all, lines_all), out_shap...  46.7 us

profile of v5, /device:TPU:1, one launch (start us, length us, event | category | flops | bytes accessed | tf_op | source)
XLA Modules:
  0.0 47.6 jit_solution(2300899654624327274)
XLA Ops:
  0.0 46.7 %shard_map.55 = bf16[2,8,80,256]{3,2,1,0:T(8,128)(2,1)S(1)} custom-call(bf16[2,8,80,256]{3,2,1,0:T(8,128)(2,1)} %features.1, bf16[2,3,3,3,256,256]{5,4,3,2,1,0:T(8,128)(2,1)} %weights.1, f32[2,256]{1,0:T(2,128)} %bias.1, f32[2,256]{1,0:T(2,128)} %gain.1, f32[2,256]{1,0:T(2,128)} %shift.1), custom_call_target="tpu_custom_call" | custom-call | flops 9059696640 | bytes 8388608 | tf_op jit(solution)/shard_map/pallas_call | solution.py:362
  46.7 0.8 %copy.7 = bf16[2,8,80,256]{3,2,1,0:T(8,128)(2,1)} copy(bf16[2,8,80,256]{3,2,1,0:T(8,128)(2,1)S(1)} %shard_map.55) | data formatting | bytes 1310720
